TPU v7x, 32 devices: a whole 2x2x4 slice. The times are simulated.
32 devices in a mesh: tensor: 2 (over core), row: 4 (over y, x), col: 4 (over z).
Axes of the slice: x: 2, y: 2, z: 4, core: 2. Of those that a mesh axis runs over, the one named last changes fastest.
Arguments:
- integral_tiles: bfloat16 [256, 8, 4096], P(('tensor', 'row', 'col')), may hold values from -6 to 6
- tile_index: int32 [256, 3], P(('tensor', 'row', 'col')), may hold values from 0 to 63, as said below
- virtual_coeff: bfloat16 [4096, 2048], P('col'), may hold values from -0.125 to 0.125
- occupied_coeff: bfloat16 [512, 512], P('row'), may hold values from -0.25 to 0.25
Outputs:
- pair_tensor: bfloat16 [2048, 32, 512], P(('row', 'col'), 'tensor')
Inputs may be any that keep to these rules, and one draw needn't show every extreme that they name: `tile_index`: the tiles of the device at index (t, r, c) of tensor, row, col all have their nu block in c * 16 .. (c + 1) * 16 - 1, their auxiliary block below 4 and their mu block below 8. A tile's owner is (tensor index a // 2, row index m // 2) in the same col. Each device holds at most 2 tiles for any one owner; in every draw some owner gets exactly 2 tiles from every device of its col. Tiles with equal indices may occur and add up.
All inputs are finite; a program needn't handle non-finite values.
Results may differ from a plain program's by a relative error of at most 0.025.
Values may be sent and summed in bfloat16 or wider, within the bound.
A program may use at most 128 MiB of HBM per device.

v0:
```python
import jax
import jax.numpy as jnp
from jax import lax
from jax.sharding import PartitionSpec as P

TB = 64
PB = 8
AB = 2
MB = 2
NBC = 16
CAP = 2
NV = 2048
NOCC = 512


def shards(integral_tiles, tile_index, virtual_coeff, occupied_coeff):
    tensor_at = lax.axis_index("tensor")
    row_at = lax.axis_index("row")
    col_at = lax.axis_index("col")
    tensor_count = lax.axis_size("tensor")
    row_count = lax.axis_size("row")
    col_count = lax.axis_size("col")
    owners = tensor_count * row_count
    held = integral_tiles.shape[0]
    tile_size = integral_tiles.shape[2]
    owner = tile_index[:, 0] // AB * row_count + tile_index[:, 1] // MB
    earlier = jnp.arange(held)[:, None] > jnp.arange(held)[None, :]
    same_owner = owner[:, None] == owner[None, :]
    rank = jnp.sum(jnp.logical_and(earlier, same_owner), axis=1)
    position = owner * CAP + rank
    slots = owners * CAP
    send_tiles = jnp.zeros((slots, PB, tile_size), jnp.bfloat16).at[position].set(integral_tiles)
    send_index = jnp.full((slots, 3), -1, jnp.int32).at[position].set(tile_index)
    recv_tiles, recv_index = (
        lax.all_to_all(
            send_tiles.reshape(owners, CAP, PB, tile_size),
            ("tensor", "row"),
            split_axis=0,
            concat_axis=0,
            tiled=True,
        ),
        lax.all_to_all(
            send_index.reshape(owners, CAP, 3),
            ("tensor", "row"),
            split_axis=0,
            concat_axis=0,
            tiled=True,
        ),
    )
    recv_tiles = recv_tiles.reshape(slots, PB * tile_size)
    recv_index = recv_index.reshape(slots, 3)
    combos = AB * MB * NBC
    valid = recv_index[:, 0] >= 0
    local_aux = recv_index[:, 0] - tensor_at * AB
    local_mu = recv_index[:, 1] - row_at * MB
    local_nu = recv_index[:, 2] - col_at * NBC
    segment = jnp.where(valid, (local_aux * MB + local_mu) * NBC + local_nu, combos)
    selector = (jnp.arange(combos)[:, None] == segment[None, :]).astype(jnp.bfloat16)
    dense = jnp.dot(selector, recv_tiles, preferred_element_type=jnp.float32).astype(jnp.bfloat16)
    dense = dense.reshape(AB, MB, NBC, PB, TB, TB)
    virt_rows = virtual_coeff.shape[0]
    per_device = NV // (row_count * col_count)
    permuted = (
        virtual_coeff.reshape(virt_rows, row_count, col_count, per_device)
        .transpose(0, 2, 1, 3)
        .reshape(NBC, TB, NV)
    )
    half_rows = AB * MB * PB * TB
    product = jnp.einsum("knv,ajkpun->vajpu", permuted, dense, preferred_element_type=jnp.float32)
    half = lax.psum_scatter(
        product.reshape(NV // col_count * lax.axis_size("col"), half_rows).astype(jnp.bfloat16),
        "col",
        scatter_dimension=0,
        tiled=True,
    )
    occ_local = occupied_coeff.reshape(MB, TB, NOCC)
    picked = half.reshape(per_device * lax.axis_size("row"), AB, MB, PB, TB)
    product = jnp.einsum("vajpu,juo->vapo", picked, occ_local, preferred_element_type=jnp.float32)
    return lax.psum_scatter(
        product.reshape(per_device * lax.axis_size("row"), AB * PB, NOCC).astype(jnp.bfloat16),
        "row",
        scatter_dimension=0,
        tiled=True,
    )


def solution(mesh):
    in_specs = (
        P(("tensor", "row", "col"), None, None),
        P(("tensor", "row", "col"), None),
        P("col", None),
        P("row", None),
    )
    out_specs = P(("row", "col"), "tensor", None)
    return jax.shard_map(shards, mesh=mesh, in_specs=in_specs, out_specs=out_specs, check_vma=False)
```

profile of v0, /device:TPU:1, one launch (start us, length us, event | category | flops | bytes accessed | tf_op | source)
XLA Modules:
  0.0 327.3 jit_solution(13240277861953012629)
XLA Ops:
  6.5 0.0 copy-start
  6.5 0.8 fusion.14
  7.3 0.8 fusion.7
  8.1 0.8 copy.23
  8.8 0.2 convert_reduce_fusion
  9.0 0.8 fusion.6
  9.8 1.2 scatter_custom_fusion
  11.0 5.2 %all-to-all-start = ((s32[8,2,3]{2,1,0:T(2,128)}), s32[8,2,3]{2,1,0:T(2,128)S(1)}, u32[]{:S(2)}, u32[]{:S(2)}) async-start(s32[8,2,3]{2,1,0:T(2,128)} %bitcast.5), calls=%async_computation | async-start | bytes 16384 | tf_op jit(solution)/shard_map/all_to_all | solution.py:42
  16.2 1.1 broadcast_in_dim.10
  17.3 2.7 scatter_fusion
  20.0 0.5 all-to-all-done
  20.5 3.9 %all-to-all-start.1 = ((bf16[8,2,8,4096]{3,2,1,0:T(8,128)(2,1)}), bf16[8,2,8,4096]{3,2,1,0:T(8,128)(2,1)S(1)}, u32[]{:S(2)}, u32[]{:S(2)}) async-start(bf16[8,2,8,4096]{3,2,1,0:T(8,128)(2,1)} %bitcast.8), calls=%async_computation.1 | async-start | bytes 2097152 | tf_op jit(solution)/shard_map/all_to_all | solution.py:35
  24.4 0.0 reduce-scatter.3.cloned.1.call-start
  24.4 7.7 %reshape.132 = bf16[1024,4,4,128]{3,2,1,0:T(4,128)(2,1)} reshape(bf16[1024,2048]{1,0:T(8,128)(2,1)} %param.6) | data formatting | bytes 8388608 | tf_op jit(solution)/shard_map/reshape | solution.py:64
  32.1 6.3 %copy.27 = bf16[1024,4,4,128]{3,2,1,0:T(4,128)(2,1)} copy(bf16[1024,4,4,128]{3,1,2,0:T(4,128)(2,1)} %bitcast.67) | data formatting | bytes 8388608 | tf_op jit(solution)/shard_map/transpose | solution.py:65
  38.3 7.8 %reshape.155 = bf16[16,64,2048,1,1,1]{2,1,0,3,4,5:T(8,128)(2,1)} reshape(bf16[1024,4,4,128]{3,2,1,0:T(4,128)(2,1)} %copy.27) | data formatting | bytes 8388608 | tf_op jit(solution)/shard_map/reshape | solution.py:66
  46.1 0.1 fusion.9
  46.2 0.1 copy.37
  46.3 0.1 copy.36
  46.4 0.1 copy.38
  46.5 0.0 all-to-all-done.1
  46.5 0.6 copy.39
  47.1 3.2 convolution_convert_fusion
  50.3 11.3 %reshape.131 = bf16[2,2,16,8,64,64]{5,4,3,2,1,0:T(8,128)(2,1)} reshape(bf16[64,32768]{1,0:T(8,128)(2,1)} %convolution_convert_fusion) | data formatting | bytes 8388608 | tf_op jit(solution)/shard_map/reshape | solution.py:60
  61.6 14.5 %bitcast_convert_fusion = bf16[2,2,8,64,2048]{4,3,2,1,0:T(8,128)(2,1)} fusion(bf16[2,2,16,8,64,64]{5,4,3,2,1,0:T(8,128)(2,1)} %reshape.131, bf16[16,64,2048,1,1,1]{2,1,0,3,4,5:T(8,128)(2,1)} %reshape.155), kind=kOutput, calls=%fused_computation.3 | convolution fusion | flops 8594128896 | bytes 16777216 | tf_op jit(solution)/shard_map/knv,ajkpun->vajpu/dot_general | solution.py:69
  76.1 0.0 reduce-scatter.3.cloned.1.call-update
  76.2 0.2 reduce-scatter.5.cloned.1.call-start
  76.4 145.3 %reduce-scatter.3.cloned.1.call-done = bf16[512,2048]{0,1:T(8,128)(2,1)} async-done(((bf16[2048,2048]{0,1:T(8,128)(2,1)}), bf16[512,2048]{0,1:T(8,128)(2,1)}) %reduce-scatter.3.cloned.1.call-update) | async-done | bytes 2097168 | tf_op jit(solution)/shard_map/reduce_scatter | solution.py:70
  221.7 1.7 copy.29
  223.4 0.0 copy-done
  223.4 5.6 %bitcast_convert_fusion.1 = bf16[512,16,512]{2,0,1:T(8,128)(2,1)} fusion(bf16[512,16,2,64]{0,3,2,1:T(8,128)(2,1)S(1)} %bitcast.69, bf16[2,64,512,1]{2,1,0,3:T(8,128)(2,1)S(1)} %bitcast.66), kind=kOutput, calls=%fused_computation.4 | convolution fusion | flops 1077936128 | bytes 10616832 | tf_op jit(solution)/shard_map/vajpu,juo->vapo/dot_general | solution.py:78
  229.0 0.0 reduce-scatter.5.cloned.1.call-update
  229.0 87.4 %reduce-scatter.5.cloned.1.call-done = bf16[128,16,512]{2,0,1:T(8,128)(2,1)} async-done(((bf16[512,16,512]{2,0,1:T(8,128)(2,1)}), bf16[128,16,512]{2,0,1:T(8,128)(2,1)}) %reduce-scatter.5.cloned.1.call-update) | async-done | bytes 2097168 | tf_op jit(solution)/shard_map/reduce_scatter | solution.py:79
  316.4 4.1 %copy.30 = bf16[128,16,512]{2,1,0:T(8,128)(2,1)} copy(bf16[128,16,512]{2,0,1:T(8,128)(2,1)} %reduce-scatter.5.cloned.1.call-done) | data formatting | bytes 4194304 | tf_op jit(solution)/shard_map/reduce_scatter | solution.py:79
  (1 shorter events, 0.0 us)
Async XLA Ops:
  6.5 216.9 %copy-start = (bf16[128,512]{1,0:T(8,128)(2,1)S(1)}, bf16[128,512]{1,0:T(8,128)(2,1)}, u32[]{:S(2)}) copy-start(bf16[128,512]{1,0:T(8,128)(2,1)} %param.7) | copy-start | bytes 393220
  11.0 9.5 %all-to-all-start = ((s32[8,2,3]{2,1,0:T(2,128)}), s32[8,2,3]{2,1,0:T(2,128)S(1)}, u32[]{:S(2)}, u32[]{:S(2)}) async-start(s32[8,2,3]{2,1,0:T(2,128)} %bitcast.5), calls=%async_computation | async-start | bytes 16384 | tf_op jit(solution)/shard_map/all_to_all | solution.py:42
  20.5 26.0 %all-to-all-start.1 = ((bf16[8,2,8,4096]{3,2,1,0:T(8,128)(2,1)}), bf16[8,2,8,4096]{3,2,1,0:T(8,128)(2,1)S(1)}, u32[]{:S(2)}, u32[]{:S(2)}) async-start(bf16[8,2,8,4096]{3,2,1,0:T(8,128)(2,1)} %bitcast.8), calls=%async_computation.1 | async-start | bytes 2097152 | tf_op jit(solution)/shard_map/all_to_all | solution.py:35
  24.4 197.3 %reduce-scatter.3.cloned.1.call-start = ((), (), s32[]{:S(2)}) async-start(), calls=%async_computation.4 | async-start | bytes 10485760 | tf_op jit(solution)/shard_map/reduce_scatter | solution.py:70
  76.2 240.3 %reduce-scatter.5.cloned.1.call-start = ((), (), s32[]{:S(2)}) async-start(), calls=%async_computation.5 | async-start | bytes 10485760 | tf_op jit(solution)/shard_map/reduce_scatter | solution.py:79
Sparse Core Ops, SparseCore 0:
  76.3 145.3 reduce-scatter.2
  229.2 87.2 reduce-scatter.4
where the time goes:
time: 329 us; the launch traced here: 327 us
  waiting for transfers between devices  233 us (71%)
  local copies, waits for them, and re-layouts  45.5 us (14%)
  matrix products  23.3 us (7%)
  between operations  13.4 us (4%)
  starting transfers between devices  9.33 us (3%)
    reduce_scatter x1, waiting for transfers between devices, shards(): lax.psum_scatter(product.reshape(NV // col_count * lax.axis_size('col'),...  145 us
    reduce_scatter x1, waiting for transfers between devices, shards(): lax.psum_scatter(product.reshape(per_device * lax.axis_size('row'), AB *...  87.4 us
    dot_general x1, matrix products, shards(): jnp.einsum('knv,ajkpun->vajpu', permuted, dense, preferred_element_type=j...  14.5 us
    reshape x1, local copies, waits for them, and re-layouts, shards(): dense = dense.reshape(AB, MB, NBC, PB, TB, TB)  11.3 us
    reshape x1, local copies, waits for them, and re-layouts, shards(): permuted = virtual_coeff.reshape(virt_rows, row_count, col_count, per_dev...  7.8 us
    reshape x1, local copies, waits for them, and re-layouts, shards(): virtual_coeff.reshape(virt_rows, row_count, col_count, per_device)  7.71 us
  transfers between devices with their start and end apart: 4, of which 3 were waited for; matrix products, arithmetic and copies ran while one was open for 8% of the time, Pallas kernels for 0%

commit v1 on v0

--- a/solution.py
+++ b/solution.py
@@ -1,6 +1,8 @@
 import jax
 import jax.numpy as jnp
 from jax import lax
+from jax.experimental import pallas as pl
+from jax.experimental.pallas import tpu as pltpu
 from jax.sharding import PartitionSpec as P
 
 TB = 64
@@ -84,6 +86,380 @@
     )
 
 
+LANES = 128
+KD = 8
+UP = TB * TB // LANES
+ROWS = PB * UP
+PAY = KD * ROWS + 16
+CUT = PAY // 32 * 16
+T, R, C = 2, 4, 4
+VB = NV // (R * C)
+NU = NBC * TB
+MESH = pl.DeviceIdType.MESH
+
+
+def gather_kernel(pay, virt, occ, tiles, coeff, occ_all, own_sem, zs, xs, ys, ss, rx, rh, rs, cs, cr, css, csr, os_, or_, oss, osr):
+    t = lax.axis_index("tensor")
+    r = lax.axis_index("row")
+    c = lax.axis_index("col")
+    sib = 1 - t
+    y = r // 2
+    x = r % 2
+    rx_ = y * 2 + (1 - x)
+    ry_ = (1 - y) * 2 + x
+    rd_ = (1 - y) * 2 + (1 - x)
+    sibling = (sib, r, c)
+    xdev = (t, rx_, c)
+    ydev = (t, ry_, c)
+    ddev = (t, rd_, c)
+
+    barrier = pltpu.get_barrier_semaphore()
+    for dev in (sibling, xdev, ydev, ddev):
+        pl.semaphore_signal(barrier, inc=1, device_id=dev, device_id_type=MESH)
+    for d in range(1, C):
+        pl.semaphore_signal(barrier, inc=1, device_id=(t, r, lax.rem(c + d, C)), device_id_type=MESH)
+    pl.semaphore_wait(barrier, 7)
+
+    def remote(src, dst, send, recv, dev):
+        return pltpu.make_async_remote_copy(
+            src_ref=src, dst_ref=dst, send_sem=send, recv_sem=recv, device_id=dev, device_id_type=MESH
+        )
+
+    def zcopy(z, way, dev, src=None):
+        slot = tiles.at[z, r, t]
+        return remote(slot if src is None else src, slot, zs.at[way, z], rx.at[z, r], dev)
+
+    def xcopy(z, src=None):
+        slot = tiles.at[z, r, t]
+        return remote(slot if src is None else src, slot, xs.at[z], rx.at[z, r], xdev)
+
+    def ycopy(z, src=None):
+        slot = tiles.at[z, r, t]
+        return remote(slot if src is None else src, slot, ys.at[z], rx.at[z, r], ydev)
+
+    def scopy(z, row, src=None):
+        slot = tiles.at[z, row, t]
+        return remote(slot if src is None else src, slot, ss.at[z, row], rs.at[z, row], sibling)
+
+    LOW, HIGH = pl.ds(0, CUT), pl.ds(CUT, PAY - CUT)
+
+    def yhalf(z):
+        slot = tiles.at[z, rx_, t, LOW]
+        return remote(slot, slot, ys.at[C + z], rh.at[0, z], ydev)
+
+    def xhalf(z):
+        slot = tiles.at[z, ry_, t, HIGH]
+        return remote(slot, slot, xs.at[C + z], rh.at[1, z], xdev)
+
+    def shalf(part, z):
+        slot = tiles.at[z, rd_, t, (LOW, HIGH)[part]]
+        return remote(slot, slot, ss.at[C + part, z], rs.at[C + part, z], sibling)
+
+    def wait_block(z, row, sem):
+        slot = tiles.at[z, row, t]
+        remote(slot, slot, zs.at[0, 0], sem, sibling).wait_recv()
+
+    def wait_half(part, z):
+        slot = tiles.at[z, rd_, t, (LOW, HIGH)[part]]
+        remote(slot, slot, zs.at[0, 0], rh.at[part, z], sibling).wait_recv()
+
+    half_nu = NU // T
+
+    def ccopy(dest):
+        return remote(
+            virt.at[pl.ds(t * half_nu, half_nu), pl.ds(pl.multiple_of((r * C + dest) * VB, VB), VB)],
+            coeff.at[c, t],
+            cs.at[dest],
+            cr.at[c],
+            (t, r, dest),
+        )
+
+    def csib(z):
+        slot = coeff.at[z, t]
+        return remote(slot, slot, css.at[z], csr.at[z], sibling)
+
+    occ_rows = occ.shape[1]
+
+    def ocopy(row, dev, at):
+        return remote(occ.at[t], occ_all.at[t, pl.ds(r * occ_rows, occ_rows)], os_.at[at], or_.at[r], dev)
+
+    def osib(row):
+        slot = occ_all.at[t, pl.ds(row * occ_rows, occ_rows)]
+        return remote(slot, slot, oss.at[row], osr.at[row], sibling)
+
+    @pl.when(c + 1 < C)
+    def _():
+        zcopy(c, 0, (t, r, c + 1), pay).start()
+
+    @pl.when(c > 0)
+    def _():
+        zcopy(c, 1, (t, r, c - 1), pay).start()
+
+    xcopy(c, pay).start()
+    ycopy(c, pay).start()
+    scopy(c, r, pay).start()
+    own = pltpu.make_async_copy(pay, tiles.at[c, r, t], own_sem.at[0])
+    own.start()
+    own_c = pltpu.make_async_copy(
+        virt.at[pl.ds(t * half_nu, half_nu), pl.ds(pl.multiple_of((r * C + c) * VB, VB), VB)],
+        coeff.at[c, t],
+        own_sem.at[1],
+    )
+    own_c.start()
+    own_o = pltpu.make_async_copy(occ.at[t], occ_all.at[t, pl.ds(r * occ_rows, occ_rows)], own_sem.at[2])
+    own_o.start()
+    own_c.wait()
+    csib(c).start()
+    own_o.wait()
+    osib(r).start()
+
+    def line_block(z):
+        xcopy(z).start()
+        ycopy(z).start()
+        scopy(z, r).start()
+
+    def plane_blocks(z):
+        wait_block(z, rx_, rx.at[z, rx_])
+        yhalf(z).start()
+        scopy(z, rx_).start()
+        wait_block(z, ry_, rx.at[z, ry_])
+        xhalf(z).start()
+        scopy(z, ry_).start()
+
+    def plane_halves(z):
+        for part in range(2):
+            wait_half(part, z)
+            shalf(part, z).start()
+
+    for d in range(1, C):
+        @pl.when(c >= d)
+        def _():
+            wait_block(c - d, r, rx.at[c - d, r])
+
+            @pl.when(c + 1 < C)
+            def _():
+                zcopy(c - d, 0, (t, r, c + 1)).start()
+
+            line_block(c - d)
+
+        @pl.when(c + d < C)
+        def _():
+            wait_block(c + d, r, rx.at[c + d, r])
+
+            @pl.when(c > 0)
+            def _():
+                zcopy(c + d, 1, (t, r, c - 1)).start()
+
+            line_block(c + d)
+
+        if d == 1:
+            for e in range(1, C):
+                ccopy(lax.rem(c + e, C)).start()
+            for at, (row, dev) in enumerate(((rx_, xdev), (ry_, ydev), (rd_, ddev))):
+                ocopy(row, dev, at).start()
+            plane_blocks(c)
+        else:
+            before = d - 1
+
+            @pl.when(c >= before)
+            def _():
+                plane_blocks(c - before)
+
+            @pl.when(c + before < C)
+            def _():
+                plane_blocks(c + before)
+
+    for e in range(1, C):
+        z = lax.rem(c + e, C)
+        remote(coeff.at[z, t], coeff.at[z, t], zs.at[0, 0], cr.at[z], sibling).wait_recv()
+        csib(z).start()
+    for row in (rx_, ry_, rd_):
+        slot = occ_all.at[t, pl.ds(row * occ_rows, occ_rows)]
+        remote(slot, slot, zs.at[0, 0], or_.at[row], sibling).wait_recv()
+        osib(row).start()
+
+    @pl.when(c >= C - 1)
+    def _():
+        plane_blocks(c - (C - 1))
+
+    @pl.when(c + C - 1 < C)
+    def _():
+        plane_blocks(c + (C - 1))
+
+    plane_halves(c)
+    for d in range(1, C):
+        @pl.when(c >= d)
+        def _():
+            plane_halves(c - d)
+
+        @pl.when(c + d < C)
+        def _():
+            plane_halves(c + d)
+
+    own.wait()
+    for z in range(C):
+        for row in (r, rx_, ry_):
+            slot = tiles.at[z, row, sib]
+            remote(slot, slot, ss.at[z, row], rs.at[z, row], sibling).wait()
+        slot = tiles.at[z, rd_, sib, LOW]
+        remote(slot, slot, ss.at[C, z], rs.at[C, z], sibling).wait()
+        slot = tiles.at[z, rd_, sib, HIGH]
+        remote(slot, slot, ss.at[C + 1, z], rs.at[C + 1, z], sibling).wait()
+        xcopy(z).wait_send()
+        ycopy(z).wait_send()
+        yhalf(z).wait_send()
+        xhalf(z).wait_send()
+
+        @pl.when(jnp.logical_and(z <= c, c + 1 < C))
+        def _():
+            zcopy(z, 0, sibling).wait_send()
+
+        @pl.when(jnp.logical_and(z >= c, c > 0))
+        def _():
+            zcopy(z, 1, sibling).wait_send()
+
+        slot = coeff.at[z, sib]
+        remote(slot, slot, css.at[z], csr.at[z], sibling).wait()
+    for e in range(1, C):
+        ccopy(lax.rem(c + e, C)).wait_send()
+    for at, (row, dev) in enumerate(((rx_, xdev), (ry_, ydev), (rd_, ddev))):
+        ocopy(row, dev, at).wait_send()
+    for row in range(R):
+        slot = occ_all.at[sib, pl.ds(row * occ_rows, occ_rows)]
+        remote(slot, slot, oss.at[row], osr.at[row], sibling).wait()
+
+
+def transform_kernel(dest, block, tiles, coeff, occ, out, diag, acc, wide):
+    step = pl.program_id(0)
+    per_step = tiles.shape[0]
+
+    @pl.when(step == 0)
+    def _():
+        acc[...] = jnp.zeros_like(acc)
+        diag[...] = jnp.zeros_like(diag)
+
+        def fill(n, _):
+            piece = coeff[n]
+            diag[n, 0:TB, 0:VB] = piece
+            diag[n, TB : 2 * TB, VB : 2 * VB] = piece
+            return 0
+
+        lax.fori_loop(0, diag.shape[0], fill, 0)
+
+    for j in range(per_step):
+        for k in range(KD):
+            at = (step * per_step + j) * KD + k
+            to = dest[at]
+
+            @pl.when(to >= 0)
+            def _():
+                part = jnp.dot(
+                    tiles[j, k * ROWS : (k + 1) * ROWS, :], diag[block[at]], preferred_element_type=jnp.float32
+                )
+                acc[0, to] += part[:, 0:VB]
+                acc[1, to] += part[:, VB : 2 * VB]
+
+    @pl.when(step == pl.num_programs(0) - 1)
+    def _():
+        mus = R * MB
+        for a in range(AB):
+            def one(p, _):
+                total = jnp.zeros((VB, NOCC), jnp.float32)
+                for low in range(2):
+                    rows = jnp.concatenate(
+                        [
+                            acc[low, a * mus + m, pl.ds(p, UP, stride=PB), :]
+                            for m in range(mus)
+                        ],
+                        axis=0,
+                    ).astype(jnp.bfloat16)
+                    total += lax.dot_general(
+                        rows, occ[low], (((0,), (0,)), ((), ())), preferred_element_type=jnp.float32
+                    )
+                for q in range(NOCC // LANES):
+                    wide[q, pl.ds(a * PB + p, VB, stride=AB * PB), :] = total[:, q * LANES : (q + 1) * LANES]
+                return 0
+
+            lax.fori_loop(0, PB, one, 0)
+
+        def put(i, _):
+            v = pl.multiple_of(i * 8, 8)
+            rows = pl.ds(pl.multiple_of(i * 8 * AB * PB, 8 * AB * PB), 8 * AB * PB)
+            for q in range(NOCC // LANES):
+                part = wide[q, rows, :].reshape(8, AB * PB, LANES).astype(jnp.bfloat16)
+                out[pl.ds(v, 8), :, q * LANES : (q + 1) * LANES] = part
+            return 0
+
+        lax.fori_loop(0, VB // 8, put, 0)
+
+
+def gathered(integral_tiles, tile_index, virtual_coeff, occupied_coeff):
+    t = lax.axis_index("tensor")
+    body = integral_tiles.reshape(KD, PB, UP, LANES).transpose(0, 2, 1, 3).reshape(KD * ROWS, LANES)
+    index = jnp.pad(tile_index.astype(jnp.bfloat16), ((0, 16 - KD), (0, LANES - 3)))
+    pay = jnp.concatenate([body, index], axis=0)
+    occ = occupied_coeff.reshape(MB * TB // 2, 2, NOCC).transpose(1, 0, 2)
+    dma = pltpu.SemaphoreType.DMA
+    tiles, coeff, occ_all = pl.pallas_call(
+        gather_kernel,
+        out_shape=(
+            jax.ShapeDtypeStruct((C, R, T, PAY, LANES), jnp.bfloat16),
+            jax.ShapeDtypeStruct((C, T, NU // T, VB), jnp.bfloat16),
+            jax.ShapeDtypeStruct((2, R * MB * TB // 2, NOCC), jnp.bfloat16),
+        ),
+        in_specs=[pl.BlockSpec(memory_space=pl.ANY)] * 3,
+        out_specs=[pl.BlockSpec(memory_space=pl.ANY)] * 3,
+        scratch_shapes=[
+            dma((3,)),
+            dma((2, C)),
+            dma((2 * C,)),
+            dma((2 * C,)),
+            dma((C + 2, R)),
+            dma((C, R)),
+            dma((2, C)),
+            dma((C + 2, R)),
+            dma((C,)),
+            dma((C,)),
+            dma((C,)),
+            dma((C,)),
+            dma((3,)),
+            dma((R,)),
+            dma((R,)),
+            dma((R,)),
+        ],
+        compiler_params=pltpu.CompilerParams(collective_id=0, has_side_effects=True),
+        name="gather_tiles",
+    )(pay, virtual_coeff, occ)
+    sources = C * R * T
+    flat = tiles.reshape(sources, PAY, LANES)
+    found = flat[:, KD * ROWS : KD * ROWS + KD, 0:3].astype(jnp.int32).reshape(sources * KD, 3)
+    aux = found[:, 0] - t * AB
+    mine = jnp.logical_and(aux >= 0, aux < AB)
+    dest = jnp.where(mine, aux * (R * MB) + found[:, 1], -1)
+    per_step = 2
+    return pl.pallas_call(
+        transform_kernel,
+        grid_spec=pltpu.PrefetchScalarGridSpec(
+            num_scalar_prefetch=2,
+            grid=(sources // per_step,),
+            in_specs=[
+                pl.BlockSpec((per_step, PAY, LANES), lambda s, *_: (s, 0, 0)),
+                pl.BlockSpec((C * NBC, TB, VB), lambda s, *_: (0, 0, 0)),
+                pl.BlockSpec((2, R * MB * TB // 2, NOCC), lambda s, *_: (0, 0, 0)),
+            ],
+            out_specs=pl.BlockSpec((VB, AB * PB, NOCC), lambda s, *_: (0, 0, 0)),
+            scratch_shapes=[
+                pltpu.VMEM((C * NBC, 2 * TB, 2 * VB), jnp.bfloat16),
+                pltpu.VMEM((2, AB * R * MB, ROWS, VB), jnp.float32),
+                pltpu.VMEM((NOCC // LANES, VB * AB * PB, LANES), jnp.float32),
+            ],
+        ),
+        out_shape=jax.ShapeDtypeStruct((VB, AB * PB, NOCC), jnp.bfloat16),
+        compiler_params=pltpu.CompilerParams(vmem_limit_bytes=40 * 1024 * 1024),
+        name="transform_tiles",
+    )(dest, found[:, 2], flat, coeff.reshape(C * NBC, TB, VB), occ_all)
+
+
 def solution(mesh):
     in_specs = (
         P(("tensor", "row", "col"), None, None),
@@ -92,4 +468,6 @@
         P("row", None),
     )
     out_specs = P(("row", "col"), "tensor", None)
-    return jax.shard_map(shards, mesh=mesh, in_specs=in_specs, out_specs=out_specs, check_vma=False)
+    sizes = tuple(mesh.shape[name] for name in ("tensor", "row", "col"))
+    body = gathered if sizes == (2, 4, 4) else shards
+    return jax.shard_map(body, mesh=mesh, in_specs=in_specs, out_specs=out_specs, check_vma=False)

time: 329 us -> 135 us (0.41)
  waiting for transfers between devices: 233 us -> 0 us
  Pallas kernels: 0 us -> 128 us
  local copies, waits for them, and re-layouts: 45.5 us -> 3.14 us
  matrix products: 23.3 us -> 0 us
  between operations: 13.4 us -> 0.05 us
  starting transfers between devices: 9.33 us -> 0 us
    reduce_scatter x2 -> x0, waiting for transfers between devices: 233 us -> none  [the longest x1 145 us: shards(): lax.psum_scatter(product.reshape(NV // col_count * lax.axis_size('col'),...]
    pallas_call x0 -> x2, Pallas kernels: none -> 128 us  [the longest x1 92.6 us: gathered(): pl.pallas_call(gather_kernel, out_shape=(jax.ShapeDtypeStruct((C, R, T, P...]
    reshape x4 -> x2, local copies, waits for them, and re-layouts: 28.6 us -> 1.62 us  [gathered(): occ = occupied_coeff.reshape(MB * TB // 2, 2, NOCC).transpose(1, 0, 2)]
    dot_general x3 -> x0, matrix products: 23.3 us -> none  [the longest x1 14.5 us: shards(): jnp.einsum('knv,ajkpun->vajpu', permuted, dense, preferred_element_type=j...]
    all_to_all x2 -> x0, starting transfers between devices: 9.1 us -> none  [the longest x1 5.22 us: shards(): lax.all_to_all(send_index.reshape(owners, CAP, 3), ('tensor', 'row'), spl...]
    transpose x1 -> x0, local copies, waits for them, and re-layouts: 6.27 us -> none  [shards(): permuted = virtual_coeff.reshape(virt_rows, row_count, col_count, per_dev...]
    reduce_scatter x1 -> x0, local copies, waits for them, and re-layouts: 4.07 us -> none  [shards(): lax.psum_scatter(product.reshape(per_device * lax.axis_size('row'), AB *...]
    scatter x2 -> x0, local copies, waits for them, and re-layouts: 3.87 us -> none  [the longest x1 2.7 us: shards(): jnp.zeros((slots, PB, tile_size), jnp.bfloat16).at[position]]
  transfers between devices with their start and end apart: 4 -> 0, of which waited for: 3 -> 0; matrix products, arithmetic and copies ran while one was open for 8% -> 0% of each run, Pallas kernels for 0% -> 0%
where the time goes in v1:
time: 135 us
  Pallas kernels  128 us (95%)
  other arithmetic  3.51 us (3%)
  local copies, waits for them, and re-layouts  3.14 us (2%)
    pallas_call x1, Pallas kernels, gathered(): pl.pallas_call(gather_kernel, out_shape=(jax.ShapeDtypeStruct((C, R, T, P...  92.6 us
    pallas_call x1, Pallas kernels, gathered(): pl.pallas_call(transform_kernel, grid_spec=pltpu.PrefetchScalarGridSpec(n...  35.7 us

profile of v1, /device:TPU:1, one launch (start us, length us, event | category | flops | bytes accessed | tf_op | source)
XLA Modules:
  0.0 135.0 jit_solution(9726741410933595948)
XLA Ops:
  0.0 0.7 convert_element_type.6
  0.7 0.1 copy.11
  0.8 1.0 reshape.35
  1.7 0.7 copy.20
  2.4 1.9 %fusion.1.pay = bf16[2064,128]{1,0:T(8,128)(2,1)} fusion(bf16[8,3]{1,0:T(8,128)(2,1)S(1)} %copy.11, bf16[2048,128]{1,0:T(8,128)(2,1)} %bitcast.23), kind=kLoop, calls=%fused_computation.2 | loop fusion | flops 1585152 | bytes 1052720 | tf_op jit(solution)/shard_map/concatenate | solution.py:400
  4.3 92.6 %gather_tiles.1 = (bf16[4,4,2,2064,128]{4,3,2,1,0:T(8,128)(2,1)}, bf16[4,2,512,128]{3,2,1,0:T(8,128)(2,1)}, bf16[2,256,512]{2,1,0:T(8,128)(2,1)}) custom-call(bf16[2064,128]{1,0:T(8,128)(2,1)} %fusion.1.pay, bf16[1024,2048]{1,0:T(8,128)(2,1)} %virt.1, bf16[2,64,512]{2,1,0:T(8,128)(2,1)} %bitcast.22), custom_call_target="tpu_custom_call" | custom-call | tf_op jit(solution)/shard_map/gather_tiles/pallas_call | solution.py:403
  96.9 0.0 copy-start
  96.9 0.9 fusion.2
  97.9 0.1 fusion.3
  98.0 0.1 copy.18
  98.1 0.1 copy.17
  98.2 0.1 copy.16
  98.3 0.0 copy-done
  98.3 0.0 copy-start.1
  98.3 1.0 copy-done.1
  99.3 35.7 %transform_tiles.1 = bf16[128,16,512]{2,1,0:T(8,128)(2,1)} custom-call(s32[256]{0:T(256)S(1)} %bitcast.19, s32[256]{0:T(256)S(1)} %bitcast.18, bf16[32,2064,128]{2,1,0:T(8,128)(2,1)} %bitcast.21, bf16[64,64,128]{2,1,0:T(8,128)(2,1)S(1)} %bitcast.17, bf16[2,256,512]{2,1,0:T(8,128)(2,1)S(1)} %copy-done.1), custom_call_target="tpu_custom_call" | custom-call | tf_op jit(solution)/shard_map/transform_tiles/pallas_call | solution.py:440
  (1 shorter events, 0.0 us)
Async XLA Ops:
  96.9 1.4 %copy-start = (bf16[4,2,512,128]{3,2,1,0:T(8,128)(2,1)S(1)}, bf16[4,2,512,128]{3,2,1,0:T(8,128)(2,1)}, u32[]{:S(2)}) copy-start(bf16[4,2,512,128]{3,2,1,0:T(8,128)(2,1)} %get-tuple-element.9) | copy-start | bytes 3145732
  98.3 1.0 copy-start.1
